TPU v7x, 512 devices: a whole 4x8x8 slice. The times are simulated.
512 devices in a mesh: layer: 128 (over z, y, x_lo), rhs: 4 (over x_hi, core).
Axes of the slice: x: 4 (x_hi: 2, x_lo: 2; x = x_hi * 2 + x_lo), y: 8, z: 8, core: 2. Of those that a mesh axis runs over, the one named last changes fastest.
Arguments:
- coupling: float32 [128, 640, 640], P('layer', 'rhs'), may hold values from -8 to 12, as said below
- density: int32 [128, 640], P('layer'), may hold values 0 or 1
- support: float32 [128, 640], P('layer'), may hold values from 0.2 to 2
- loads: float32 [128, 640, 1024], P('layer', None, 'rhs'), may hold values from -6 to 6
Outputs:
- reduced_diag: float32 [128, 640, 640], P('layer', 'rhs')
- reduced_lower: float32 [128, 640, 640], P('layer', 'rhs')
- reduced_upper: float32 [128, 640, 640], P('layer', 'rhs')
- reduced_loads: float32 [128, 640, 1024], P('layer', None, 'rhs')
Inputs may be any that keep to these rules, and one draw needn't show every extreme that they name: Each coupling block is symmetric and positive definite.
All inputs are finite; a program needn't handle non-finite values. No bound on the sum of `density` on one device may be relied on, other than what follows from the above.
Results may differ from a plain program's by a relative error of at most 0.0003.
Values sent between devices are 32-bit elements; how exact they have to be, the bound alone decides.
No kernel may reach another device: no remote copies, remote signals or barrier semaphores. Data moves between devices by JAX's collectives and lax.ppermute only.
A program may use at most 64 MiB of HBM per device.

v0:
```python
import functools

import jax
import jax.numpy as jnp
from jax import lax
from jax.experimental import pallas as pl
from jax.experimental.pallas import tpu as pltpu
from jax.sharding import PartitionSpec as P

TILE = 128
ROWS = 8
AXES = ("layer", "rhs")
VMEM_BYTES = 28 * 1024 * 1024


def split3(x):
    high = x.astype(jnp.bfloat16)
    rest = x - high.astype(jnp.float32)
    mid = rest.astype(jnp.bfloat16)
    low = (rest - mid.astype(jnp.float32)).astype(jnp.bfloat16)
    return high, mid, low


def bdot(a, b):
    return jnp.dot(a, b, preferred_element_type=jnp.float32)


def thin_matmul(a, b):
    ah, am, al = split3(a)
    bh, bm, bl = split3(b)
    small = bdot(jnp.concatenate([ah, al], 1), jnp.concatenate([bl, bh], 0))
    mid = bdot(jnp.concatenate([ah, am], 1), jnp.concatenate([bm, bm], 0))
    top = bdot(jnp.concatenate([ah, am], 1), jnp.concatenate([bh, bh], 0))
    return top + (mid + small)


def six_pass(a, b, across=False):
    ah, am, al = split3(a)
    bh, bm, bl = split3(b)
    left = jnp.concatenate([al, ah, am, am, ah, ah], 1)
    side = 1 if across else 0
    right = jnp.concatenate([bh, bl, bm, bh, bm, bh], side)
    return lax.dot_general(
        left, right, (((1,), (side,)), ((), ())), preferred_element_type=jnp.float32
    )


def split2(x):
    high = x.astype(jnp.bfloat16)
    return high, (x - high.astype(jnp.float32)).astype(jnp.bfloat16)


def three_pass(a, b, across=False):
    ah, al = split2(a)
    bh, bl = split2(b)
    left = jnp.concatenate([al, ah, ah], 1)
    side = 1 if across else 0
    right = jnp.concatenate([bh, bl, bh], side)
    return lax.dot_general(
        left, right, (((1,), (side,)), ((), ())), preferred_element_type=jnp.float32
    )


def lanes(x, j):
    return jnp.broadcast_to(x[:, j : j + 1], (ROWS, TILE))


def subs(x, j):
    return jnp.broadcast_to(x[j : j + 1, :], (ROWS, TILE))


def tree_sum(terms):
    terms = list(terms)
    while len(terms) > 1:
        terms = [sum(terms[i : i + 2][1:], terms[i]) for i in range(0, len(terms), 2)]
    return terms[0]


def short_matmul(a, b):
    ah, am, al = split3(a)
    bh, bm, bl = split3(b)
    return bdot(
        jnp.concatenate([al, ah, am, am, ah, ah], 1), jnp.concatenate([bh, bl, bm, bh, bm, bh], 0)
    )


GROUP = 2


def invert_tile(block):
    count = TILE // ROWS
    span = GROUP * ROWS
    rows = [block[ROWS * i : ROWS * i + ROWS, :] for i in range(count)]
    lane = lax.broadcasted_iota(jnp.int32, (ROWS, TILE), 1)
    sub = lax.broadcasted_iota(jnp.int32, (ROWS, TILE), 0)
    units = [jnp.where(sub == t, jnp.float32(1.0), jnp.float32(0.0)) for t in range(ROWS)]
    b = [lanes(rows[0], j) for j in range(ROWS)]
    for first in range(0, count, GROUP):
        now = list(range(first, first + GROUP))
        soon = [i for i in range(first + GROUP, first + 2 * GROUP) if i < count]
        rest = [i for i in range(count) if i not in now and i not in soon]
        before = list(rows)
        for p in now:
            k = ROWS * p
            inside = (lane >= k) & (lane < k + ROWS)
            r = rows[p]
            ahead = []
            if p + 1 < count:
                ahead = [lanes(r, k + ROWS + j) for j in range(ROWS)]
                below = [lanes(rows[p + 1], k + j) for j in range(ROWS)]
                beyond = [lanes(rows[p + 1], k + ROWS + j) for j in range(ROWS)]
            r = jnp.where(inside, jnp.where(lane - k == sub, jnp.float32(1.0), jnp.float32(0.0)), r)
            for t in range(0, ROWS, 2):
                top = subs(b[t], t)
                side = subs(b[t + 1], t)
                low = subs(b[t + 1], t + 1)
                inverse = 1.0 / (top * low - side * side)
                f = (b[t] - units[t]) * (1.0 / top)
                w = ((b[t + 1] - f * side) - units[t + 1]) * top
                g = w * inverse

                def eliminate(x, hurry=False):
                    x = x - f * subs(x, t)
                    other = subs(x, t + 1)
                    return x - ((w * other) * inverse if hurry else g * other)

                for j in range(t + 2, ROWS):
                    b[j] = eliminate(b[j], j < t + 4)
                r = eliminate(r)
                ahead = [eliminate(x) for x in ahead]
            if ahead:
                b = [
                    beyond[j] - tree_sum(below[m] * subs(ahead[j], m) for m in range(ROWS))
                    for j in range(ROWS)
                ]
            q = [subs(r, j) for j in range(ROWS)]
            for i in [i for i in now + soon if i > p] + [i for i in now if i < p]:
                e = rows[i]
                spread = below if i == p + 1 else [lanes(e, k + j) for j in range(ROWS)]
                kept = jnp.where(inside, jnp.float32(0.0), e)
                rows[i] = kept - tree_sum(spread[j] * q[j] for j in range(ROWS))
            rows[p] = r
        start = first * ROWS
        solved = jnp.concatenate([rows[i] for i in now], 0)
        for part in ([i for i in rest if i > first], [i for i in rest if i < first]):
            if part:
                c = jnp.concatenate([before[i] for i in part], 0)
                wide = lax.broadcasted_iota(jnp.int32, c.shape, 1)
                done = (wide >= start) & (wide < start + span)
                update = short_matmul(c[:, start : start + span], solved)
                c = jnp.where(done, jnp.float32(0.0), c) - update
                for m, i in enumerate(part):
                    rows[i] = c[ROWS * m : ROWS * m + ROWS, :]
    return jnp.concatenate(rows, 0)


def sweep(a_ref, block, row_start):
    col_start = pl.multiple_of(block * TILE, TILE)
    row_start = pl.multiple_of(row_start, 64)
    rows = pl.ds(row_start, TILE)
    cols = pl.ds(col_start, TILE)
    inverse = invert_tile(a_ref[rows, cols])
    solved = thin_matmul(inverse, a_ref[rows, :])
    column = a_ref[:, cols]
    a_ref[:, cols] = jnp.zeros_like(column)
    lane = lax.broadcasted_iota(jnp.int32, solved.shape, 1)
    inside = (lane >= col_start) & (lane < col_start + TILE)
    tiled = jnp.concatenate([inverse] * (solved.shape[1] // TILE), axis=1)
    solved = jnp.where(inside, tiled, solved)
    a_ref[...] = a_ref[...] - thin_matmul(column, solved)
    a_ref[rows, :] = solved


SMEM = pl.BlockSpec(memory_space=pltpu.SMEM)
VMEM = pl.BlockSpec(memory_space=pltpu.VMEM)
HALF, CORE, LIVE, LIVE_FAR, LONE = range(5)


def local_call(body, name, micros, flags, inputs, shapes, scratch=()):
    out = pl.pallas_call(
        body,
        out_shape=[jax.ShapeDtypeStruct(shape, jnp.float32) for shape in shapes],
        in_specs=[SMEM] + [VMEM] * len(inputs),
        out_specs=[VMEM] * len(shapes),
        scratch_shapes=[pltpu.VMEM(shape, jnp.float32) for shape in scratch],
        compiler_params=pltpu.CompilerParams(vmem_limit_bytes=VMEM_BYTES),
        cost_estimate=pl.CostEstimate(
            flops=int(micros * 1.1e9), transcendentals=0, bytes_accessed=int(micros * 3.5e6)
        ),
        name=name,
    )(flags, *inputs)
    return out


def rows_of(half, size):
    return pl.ds(pl.multiple_of(half * size, 64), size)


def lone_diag(flags, offset, shape):
    row = lax.broadcasted_iota(jnp.int32, shape, 0) + offset
    col = lax.broadcasted_iota(jnp.int32, shape, 1)
    lone = jnp.where(flags[LONE] == 1, jnp.float32(1.0), jnp.float32(0.0))
    return jnp.where(row == col, lone, jnp.float32(0.0))


def factor_of(flag):
    return jnp.where(flag == 1, jnp.float32(1.0), jnp.float32(0.0))


def first_kernel(flags, own_ref, out_ref):
    half = flags[HALF]
    size = own_ref.shape[0]
    out_ref[...] = own_ref[...] + lone_diag(flags, half * size, own_ref.shape)

    def body(step, carry):
        block = jnp.where(half == 0, step, 4 - step)
        sweep(out_ref, block, block * TILE - half * size)
        return carry

    lax.fori_loop(0, 2, body, 0)


def complete(half, own_ref, square, turned_ref, full_ref):
    size = own_ref.shape[0]
    own = own_ref[...]
    turned_ref[...] = own.T
    full_ref[rows_of(half, size), :] = own

    @pl.when(half == 0)
    def _():
        full_ref[size:, :size] = turned_ref[size:, :]
        full_ref[size:, size:] = square

    @pl.when(half == 1)
    def _():
        full_ref[:size, size:] = turned_ref[:size, :]
        full_ref[:size, :size] = square


def second_kernel(first_col, flags, own_ref, swept_ref, square_ref, out_ref, turned_ref):
    half = flags[HALF]
    size = own_ref.shape[0]
    square = square_ref[:, first_col : first_col + size]
    complete(half, own_ref, square, turned_ref, out_ref)
    other_rows = rows_of(1 - half, size)
    done_cols = pl.multiple_of(half * 384, TILE)
    column = out_ref[other_rows, pl.ds(done_cols, 256)]
    solved = swept_ref[pl.ds(pl.multiple_of(half * 64, 64), 256), :]
    shape = own_ref.shape
    lane = lax.broadcasted_iota(jnp.int32, shape, 1)
    done = (lane >= done_cols) & (lane < done_cols + 256)
    other = out_ref[other_rows, :] + lone_diag(flags, (1 - half) * size, shape)
    out_ref[rows_of(half, size), :] = swept_ref[...]
    out_ref[other_rows, :] = jnp.where(done, jnp.float32(0.0), other) - six_pass(column, solved)

    def body(step, carry):
        block = jnp.where(half == 0, 2 + step, 2 - step)
        sweep(out_ref, block, block * TILE)
        return carry

    lax.fori_loop(0, 3, body, 0)


def rest_kernel(flags, inverse_ref, x_ref, square_ref, g_ref, rest_ref, turned_ref, full_ref):
    half = flags[HALF]
    size, width = x_ref.shape
    complete(half, x_ref, square_ref[...], turned_ref, full_ref)
    g_ref[...] = factor_of(flags[LIVE]) * six_pass(full_ref[...], inverse_ref[...])
    own_rows, other_rows = rows_of(half, size), rows_of(1 - half, size)
    rest_ref[:, :width] = x_ref[...] - six_pass(g_ref[own_rows, :], full_ref[...])
    rest_ref[:, width : width + size] = square_ref[...] - six_pass(
        g_ref[other_rows, :], full_ref[other_rows, :], across=True
    )
    rest_ref[:, width + size :] = jnp.zeros_like(rest_ref[:, width + size :])


def link_kernel(flags, g_ref, y_ref, y_square_ref, link_ref, turned_link_ref, turned_ref, full_ref):
    complete(flags[HALF], y_ref, y_square_ref[...], turned_ref, full_ref)
    live = -factor_of(flags[LIVE_FAR])
    g = g_ref[...]
    link_ref[...] = live * three_pass(g, full_ref[...])
    turned_link_ref[...] = live * three_pass(y_ref[...], g, across=True)


def combine_kernel(flags, rest_ref, came_ref, diag_ref, link_ref, own_out, packed_out):
    size, width = own_out.shape
    row = lax.broadcasted_iota(jnp.int32, (size, width), 0) + flags[HALF] * size
    col = lax.broadcasted_iota(jnp.int32, (size, width), 1)
    own_diag = jnp.where(row == col, diag_ref[:, :width], jnp.float32(0.0))
    own_out[...] = rest_ref[:, :width] + came_ref[:, :width] + own_diag
    tail = rest_ref.shape[1] - width
    row = lax.broadcasted_iota(jnp.int32, (size, tail), 0)
    col = lax.broadcasted_iota(jnp.int32, (size, tail), 1)
    square_diag = jnp.where(row == col, diag_ref[:, width:], jnp.float32(0.0))
    packed_out[:, :width] = link_ref[...]
    packed_out[:, width:] = rest_ref[:, width:] + came_ref[:, width:] + square_diag


def near_kernel(flags, g_ref, loads_ref, part_ref):
    part_ref[...] = three_pass(g_ref[...], loads_ref[...])


def post_kernel(flags, inverse_ref, link_ref, far_ref, diag_ref, g_ref, kept_ref, sent_ref, part_ref):
    half, core = flags[HALF], flags[CORE]
    size, width = diag_ref.shape
    link = link_ref[...]
    both = three_pass(jnp.concatenate([link, far_ref[:, :width]], 0), inverse_ref[...])
    g_ref[...] = both[:width]
    left = jnp.concatenate([g_ref[rows_of(half, size), :], both[width:]], 0)
    part_ref[...] = three_pass(left, link, across=True)
    part = size // 2
    keep = pl.multiple_of(core * part, 32)
    send = pl.multiple_of((1 - core) * part, 32)
    kept_ref[:part, :] = diag_ref[pl.ds(keep, part), :] - part_ref[pl.ds(keep, part), :]
    kept_ref[part:, :] = -part_ref[pl.ds(size + keep, part), :]
    sent_ref[:part, :] = -part_ref[pl.ds(send, part), :]
    sent_ref[part:, :] = -part_ref[pl.ds(size + send, part), :]


def last_kernel(flags, g_ref, loads_ref, near_ref, kept_ref, sent_ref, part_ref):
    core = flags[CORE]
    width = kept_ref.shape[1]
    part_ref[...] = three_pass(g_ref[...], near_ref[...])
    keep = pl.ds(pl.multiple_of(core * width, width), width)
    send = pl.ds(pl.multiple_of((1 - core) * width, width), width)
    kept_ref[...] = loads_ref[:, keep] - part_ref[:, keep]
    sent_ref[...] = -part_ref[:, send]


def device(layer, half, core):
    return layer * 4 + half * 2 + core


def pairs_of(count, moves):
    pairs = []
    for layer in range(count):
        for half in range(2):
            for core, up, across, onto in moves:
                if 0 <= layer + up < count:
                    pairs.append(
                        (device(layer, half, core), device(layer + up, half ^ across, onto))
                    )
    return pairs


def after(array, *others):
    return lax.optimization_barrier((array,) + others)[0]


def shards(coupling, density, support, loads):
    part = coupling.shape[1]
    width = coupling.shape[2]
    layers = lax.axis_size("layer")
    layer = lax.axis_index("layer")
    place = lax.axis_index("rhs")
    half = place // 2
    core = place % 2
    upper = core == 1

    def move(array, *moves):
        return lax.ppermute(array, AXES, pairs_of(layers, moves))

    def straight(array, by):
        return move(array, (0, by, 0, 0), (1, -by, 0, 1))

    def crossed(array, by):
        return move(array, (1, by, 0, 0), (0, -by, 0, 1))

    def sibling(array):
        return move(array, (0, 0, 0, 1), (1, 0, 0, 0))

    def opposite(array):
        return move(array, (0, 0, 1, 0), (1, 0, 1, 1))

    def pick(on_upper, on_lower):
        return jnp.where(upper, on_upper, on_lower)

    span = 2 * part
    cases = loads.shape[2]

    def square(array, first):
        return jnp.where(first == 0, array[:, :span], array[:, span:])

    live = jnp.logical_not(upper & (layer == layers - 1))
    live_far = jnp.logical_not(upper & (layer == layers - 2))
    lone = jnp.logical_not(pick(layer + 2 < layers, layer >= 2))
    zero = jnp.zeros((), jnp.int32)
    flags_0 = jnp.stack([half, core, live, live_far, zero]).astype(jnp.int32)
    flags_1 = jnp.stack([half, core, live, live_far, lone]).astype(jnp.int32)
    row = lax.broadcasted_iota(jnp.int32, (span, width), 0)
    col = lax.broadcasted_iota(jnp.int32, (span, width), 1)
    own_diag = col == row + half * span
    square_diag = row[:, :span] == col[:, :span]

    rho = 0.3 + 0.7 * density[0].astype(jnp.float32)
    rho_rows = lax.dynamic_slice_in_dim(rho, place * part, part, 0)
    stiff = rho_rows[:, None] * coupling[0] * rho[None, :]
    ones = jnp.ones((ROWS - 1, width), jnp.float32)
    tagged = jnp.concatenate([stiff, support, ones], axis=0)

    near_a = straight(tagged, 1)
    near_b = crossed(stiff, 1)
    far_a = move(stiff, (0, 2, 0, 0))
    far_b = move(stiff, (1, 2, 0, 0), (0, 0, 0, 1))
    side_support = jnp.where(near_a[part + 1] > 0.5, near_a[part], jnp.float32(1.0))
    near_a = near_a[:part]
    x_own = jnp.concatenate([pick(far_b, near_a), pick(stiff, near_b)], axis=0)
    y_own = jnp.concatenate([pick(near_b, far_a), pick(near_a, far_b)], axis=0)
    d_own = (x_own + y_own) + jnp.where(own_diag, side_support[None, :], jnp.float32(0.0))

    d_square = opposite(square(d_own, half))
    own_shape = (span, width)
    full_shape = (width, width)
    packed_shape = (span, width + 3 * TILE)
    load_shape = (width, cases)
    pair_shape = (width, 2 * cases)
    turned_shape = (width, span)

    loads_0 = loads[0]
    loads_in = sibling(loads_0)
    loads_0 = jnp.concatenate([pick(loads_in, loads_0), pick(loads_0, loads_in)], axis=1)
    (swept_0,) = local_call(first_kernel, "invert_first", 9, flags_0, [d_own], [own_shape])
    x_square = opposite(after(square(x_own, half), swept_0))
    near_loads = straight(after(loads_0, swept_0), 1)
    (inverse,) = local_call(
        functools.partial(second_kernel, 0), "invert_second", 14, flags_0,
        [d_own, swept_0, d_square], [full_shape], [turned_shape],
    )
    g_full, rest = local_call(
        rest_kernel, "rest", 1, flags_0, [inverse, x_own, x_square],
        [full_shape, packed_shape], [turned_shape, full_shape],
    )
    rest_in = sibling(rest)
    other_side = jnp.where(half == 0, side_support[span:], side_support[:span])
    y_square = (d_square - x_square) - jnp.where(square_diag, other_side[None, :], jnp.float32(0.0))
    link, turned_link = local_call(
        link_kernel, "links", 5, flags_0, [g_full, after(y_own, near_loads), y_square],
        [full_shape, own_shape], [turned_shape, full_shape],
    )
    other_support = jnp.where(half == 0, support[:, span:], support[:, :span])
    rest_diag = jnp.concatenate([support, other_support, jnp.zeros((1, 3 * TILE - span))], axis=1)
    new_own, packed = local_call(
        combine_kernel, "combine", 1, flags_0, [rest, rest_in, rest_diag, turned_link],
        [own_shape, packed_shape],
    )
    d_own = straight(new_own, 2)
    packed = straight(packed, 2)
    (near_part,) = local_call(
        near_kernel, "near_loads", 2, flags_0, [after(g_full, new_own), near_loads], [pair_shape]
    )
    new_loads = loads_0 + near_part + sibling(near_part)

    (swept,) = local_call(first_kernel, "invert_first", 9, flags_1, [d_own], [own_shape])
    near_loads = straight(after(new_loads, swept), 2)
    (inverse,) = local_call(
        functools.partial(second_kernel, width), "invert_second", 14, flags_1,
        [d_own, swept, packed], [full_shape], [turned_shape],
    )
    g_full, kept, sent = local_call(
        post_kernel, "last_blocks", 6, flags_1, [inverse, link, packed, new_own],
        [full_shape, own_shape, own_shape], [full_shape],
    )
    came = sibling(sent)
    load_kept, load_sent = local_call(
        last_kernel, "last_loads", 2, flags_1, [g_full, new_loads, near_loads],
        [load_shape, load_shape], [pair_shape],
    )
    loads_out = load_kept + sibling(load_sent)
    diag_out = kept[:part] + came[:part]
    lower_out = pick(came[part:], kept[part:])
    upper_out = pick(kept[part:], came[part:])
    return (diag_out[None], lower_out[None], upper_out[None], loads_out[None])


def solution(mesh):
    placed = (P("layer", "rhs", None), P("layer", None), P("layer", None), P("layer", None, "rhs"))
    return jax.shard_map(
        shards,
        mesh=mesh,
        in_specs=placed,
        out_specs=(
            P("layer", "rhs", None),
            P("layer", "rhs", None),
            P("layer", "rhs", None),
            P("layer", None, "rhs"),
        ),
        check_vma=False,
    )
```

profile of v0, /device:TPU:251, one launch (start us, length us, event | category | flops | bytes accessed | tf_op | source)
XLA Modules:
  0.0 159.6 jit_solution(16868979899886578759)
XLA Ops:
  0.6 0.0 copy-start.6
  0.7 0.8 multiply_add_fusion
  1.4 0.1 constant_dynamic-slice_fusion
  1.5 1.1 fusion.4
  2.6 1.4 collective-permute-start.3
  4.1 7.0 %collective-permute-start.2 = (f32[160,640]{1,0:T(8,128)S(1)}, f32[160,640]{1,0:T(8,128)}, u32[]{:S(2)}, u32[]{:S(2)}) collective-permute-start(f32[160,640]{1,0:T(8,128)S(1)} %fusion.4), channel_id=1, source_target_pairs={{1,4},{3,6},{5,8},{4,1},{7,10},{6,3},{9,12},{8,5},{11,14},{10,7},{... | collective-permute-start | bytes 1228808 | tf_op jit(solution)/shard_map/ppermute | solution.py:361
  11.1 0.1 pad.11.clone
  11.2 0.8 maximum_maximum_fusion
  12.0 2.1 %collective-permute-start.1 = (f32[168,640]{1,0:T(8,128)S(1)}, f32[168,640]{1,0:T(8,128)}, u32[]{:S(2)}, u32[]{:S(2)}) collective-permute-start(f32[168,640]{1,0:T(8,128)S(1)} %maximum_maximum_fusion), channel_id=1, source_target_pairs={{0,4},{2,6},{4,8},{5,1},{6,10},{7,3},{8,12},{9,5},{10,14},{11,7},{... | collective-permute-start | bytes 1290248 | tf_op jit(solution)/shard_map/ppermute | solution.py:361
  14.1 3.3 %collective-permute-start = (f32[160,640]{1,0:T(8,128)S(1)}, f32[160,640]{1,0:T(8,128)S(1)}, u32[]{:S(2)}, u32[]{:S(2)}) collective-permute-start(f32[160,640]{1,0:T(8,128)S(1)} %fusion.4), channel_id=1, source_target_pairs={{1,8},{0,1},{3,10},{2,3},{5,12},{4,5},{7,14},{6,7},{9,16},{8,9},{1... | collective-permute-start | bytes 1228808 | tf_op jit(solution)/shard_map/ppermute | solution.py:361
  17.4 1.9 %collective-permute-start.7 = (f32[640,256]{1,0:T(8,128)S(1)}, f32[640,256]{1,0:T(8,128)S(1)}, u32[]{:S(2)}, u32[]{:S(2)}) collective-permute-start(f32[640,256]{1,0:T(8,128)S(1)} %bitcast.24), channel_id=1, source_target_pairs={{0,1},{1,0},{2,3},{3,2},{4,5},{5,4},{6,7},{7,6},{8,9},{9,8},{10,11... | collective-permute-start | bytes 1966088 | tf_op jit(solution)/shard_map/ppermute | solution.py:361
  19.4 0.1 pad.4.clone
  19.4 0.1 stack.43.flags
  19.5 0.0 collective-permute-done.3
  19.5 1.1 broadcast_select_fusion.3
  20.7 5.8 %collective-permute-done = f32[160,640]{1,0:T(8,128)S(1)} collective-permute-done((f32[160,640]{1,0:T(8,128)S(1)}, f32[160,640]{1,0:T(8,128)S(1)}, u32[]{:S(2)}, u32[]{:S(2)}) %collective-permute-start) | collective-permute-done | bytes 409632 | tf_op jit(solution)/shard_map/ppermute | solution.py:361
  26.5 2.1 %collective-permute-done.1 = f32[168,640]{1,0:T(8,128)} collective-permute-done((f32[168,640]{1,0:T(8,128)S(1)}, f32[168,640]{1,0:T(8,128)}, u32[]{:S(2)}, u32[]{:S(2)}) %collective-permute-start.1) | collective-permute-done | bytes 430112 | tf_op jit(solution)/shard_map/ppermute | solution.py:361
  28.6 1.1 slice_select_fusion.2
  29.7 0.2 fusion.1
  29.9 0.8 fusion.7
  30.7 0.2 pad_maximum_fusion.2
  30.9 0.2 slice_select_fusion
  31.1 3.8 %collective-permute-start.4 = (f32[320,320]{1,0:T(8,128)S(1)}, f32[320,320]{1,0:T(8,128)S(1)}, u32[]{:S(2)}, u32[]{:S(2)}) collective-permute-start(f32[320,320]{1,0:T(8,128)S(1)} %slice_select_fusion), channel_id=1, source_target_pairs={{0,2},{1,3},{2,0},{3,1},{4,6},{5,7},{6,4},{7,5},{8,10},{9,11},{10,... | collective-permute-start | bytes 1228808 | tf_op jit(solution)/shard_map/ppermute | solution.py:361
  34.9 8.0 %invert_first.2.swept_ref = f32[320,640]{1,0:T(8,128)S(1)} custom-call(s32[5]{0:T(128)S(1)} %stack.43.flags, f32[320,640]{1,0:T(8,128)S(1)} %get-tuple-element.46.own_ref), custom_call_target="tpu_custom_call" | custom-call | flops 9900000256 | bytes 31500000 | tf_op jit(solution)/shard_map/invert_first/pallas_call | solution.py:180
  42.9 3.0 %collective-permute-start.5 = (f32[320,320]{1,0:T(8,128)S(1)}, f32[320,320]{1,0:T(8,128)S(1)}, u32[]{:S(2)}, u32[]{:S(2)}) collective-permute-start(f32[320,320]{1,0:T(8,128)S(1)} %fusion.1), channel_id=1, source_target_pairs={{0,2},{1,3},{2,0},{3,1},{4,6},{5,7},{6,4},{7,5},{8,10},{9,11},{10,... | collective-permute-start | bytes 1228808 | tf_op jit(solution)/shard_map/ppermute | solution.py:361
  46.0 0.0 collective-permute-done.7
  46.0 0.1 broadcast_select_fusion.1
  46.1 0.0 copy-start.4
  46.1 0.1 pad_maximum_fusion
  46.2 0.7 copy-done.2
  46.9 0.2 copy-done.4
  47.1 3.9 %collective-permute-start.8 = (f32[640,512]{1,0:T(8,128)S(1)}, f32[640,512]{1,0:T(8,128)S(1)}, u32[]{:S(2)}, u32[]{:S(2)}) collective-permute-start(f32[640,512]{1,0:T(8,128)S(1)} %pad_maximum_fusion), channel_id=1, source_target_pairs={{0,4},{2,6},{4,8},{5,1},{6,10},{7,3},{8,12},{9,5},{10,14},{11,7},{... | collective-permute-start | bytes 3932168 | tf_op jit(solution)/shard_map/ppermute | solution.py:361
  51.0 0.0 collective-permute-done.4.square_ref
  51.0 14.3 %invert_second.2.inverse_ref = f32[640,640]{1,0:T(8,128)S(1)} custom-call(s32[5]{0:T(128)S(1)} %stack.43.flags, f32[320,640]{1,0:T(8,128)S(1)} %get-tuple-element.46.own_ref, f32[320,640]{1,0:T(8,128)S(1)} %invert_first.2.swept_ref, f32[320,320]{1,0:T(8,128)S(1)} %collective-permute-done.4.square_ref), custom_call_target="tpu_custom_call" | custom-call | flops 15399999488 | bytes 49000000 | tf_op jit(solution)/shard_map/invert_second/pallas_call | solution.py:180
  65.4 5.0 %collective-permute-done.5.square_ref = f32[320,320]{1,0:T(8,128)S(1)} collective-permute-done((f32[320,320]{1,0:T(8,128)S(1)}, f32[320,320]{1,0:T(8,128)S(1)}, u32[]{:S(2)}, u32[]{:S(2)}) %collective-permute-start.5) | collective-permute-done | bytes 409632 | tf_op jit(solution)/shard_map/ppermute | solution.py:361
  70.4 9.9 %rest.1 = (f32[640,640]{1,0:T(8,128)S(1)}, f32[320,1024]{1,0:T(8,128)S(1)}) custom-call(s32[5]{0:T(128)S(1)} %stack.43.flags, f32[640,640]{1,0:T(8,128)S(1)} %invert_second.2.inverse_ref, f32[320,640]{1,0:T(8,128)S(1)} %get-tuple-element.47.x_ref, f32[320,320]{1,0:T(8,128)S(1)} %collective-permute-done.5.square_ref), custom_call_target="tpu_custom_call" | custom-call | flops 1100000000 | bytes 3500000 | tf_op jit(solution)/shard_map/rest/pallas_call | solution.py:180
  80.3 8.7 %collective-permute-start.6 = (f32[320,1024]{1,0:T(8,128)S(1)}, f32[320,1024]{1,0:T(8,128)S(1)}, u32[]{:S(2)}, u32[]{:S(2)}) collective-permute-start(f32[320,1024]{1,0:T(8,128)S(1)} %get-tuple-element.21.rest_ref), channel_id=1, source_target_pairs={{0,1},{1,0},{2,3},{3,2},{4,5},{5,4},{6,7},{7,6},{8,9},{9,8},{10,11... | collective-permute-start | bytes 3932168 | tf_op jit(solution)/shard_map/ppermute | solution.py:361
  89.0 0.1 broadcast_select_fusion.5
  89.1 0.1 fusion.5
  89.2 0.1 select_subtract_fusion.y_square_ref
  89.3 4.2 %links.1 = (f32[640,640]{1,0:T(8,128)S(1)}, f32[320,640]{1,0:T(8,128)S(1)}) custom-call(s32[5]{0:T(128)S(1)} %stack.43.flags, f32[640,640]{1,0:T(8,128)S(1)} %get-tuple-element.32.g_ref, f32[320,640]{1,0:T(8,128)S(1)} %get-tuple-element.24.y_ref, f32[320,320]{1,0:T(8,128)S(1)} %select_subtract_fusion.y_square_ref), custom_call_target="tpu_custom_call" | custom-call | flops 5500000256 | bytes 17500000 | tf_op jit(solution)/shard_map/links/pallas_call | solution.py:180
  93.5 0.0 collective-permute-done.6.came_ref
  93.5 0.7 combine.1
  94.3 0.4 copy-done
  94.7 1.9 %collective-permute-start.9 = (f32[320,640]{1,0:T(8,128)S(1)}, f32[320,640]{1,0:T(8,128)}, u32[]{:S(2)}, u32[]{:S(2)}) collective-permute-start(f32[320,640]{1,0:T(8,128)S(1)} %get-tuple-element.26.diag_ref), channel_id=1, source_target_pairs={{0,8},{2,10},{4,12},{6,14},{8,16},{9,1},{10,18},{11,3},{12,20},{13... | collective-permute-start | bytes 2457608 | tf_op jit(solution)/shard_map/ppermute | solution.py:361
  96.7 2.1 %near_loads.1 = f32[640,512]{1,0:T(8,128)S(1)} custom-call(s32[5]{0:T(128)S(1)} %stack.43.flags, f32[640,640]{1,0:T(8,128)S(1)} %get-tuple-element.32.g_ref, f32[640,512]{1,0:T(8,128)S(1)} %collective-permute-done.8.loads_ref), custom_call_target="tpu_custom_call" | custom-call | flops 2200000000 | bytes 7000000 | tf_op jit(solution)/shard_map/near_loads/pallas_call | solution.py:180
  98.7 4.0 %collective-permute-start.12 = (f32[640,512]{1,0:T(8,128)S(1)}, f32[640,512]{1,0:T(8,128)}, u32[]{:S(2)}, u32[]{:S(2)}) collective-permute-start(f32[640,512]{1,0:T(8,128)S(1)} %near_loads.1), channel_id=1, source_target_pairs={{0,1},{1,0},{2,3},{3,2},{4,5},{5,4},{6,7},{7,6},{8,9},{9,8},{10,11... | collective-permute-start | bytes 3932168 | tf_op jit(solution)/shard_map/ppermute | solution.py:361
  102.7 2.1 %collective-permute-start.10 = (f32[320,1024]{1,0:T(8,128)S(1)}, f32[320,1024]{1,0:T(8,128)}, u32[]{:S(2)}, u32[]{:S(2)}) collective-permute-start(f32[320,1024]{1,0:T(8,128)S(1)} %get-tuple-element.27), channel_id=1, source_target_pairs={{0,8},{2,10},{4,12},{6,14},{8,16},{9,1},{10,18},{11,3},{12,20},{13... | collective-permute-start | bytes 3932168 | tf_op jit(solution)/shard_map/ppermute | solution.py:361
  104.9 0.1 stack.42.flags
  105.0 6.3 %collective-permute-done.9.own_ref = f32[320,640]{1,0:T(8,128)} collective-permute-done((f32[320,640]{1,0:T(8,128)S(1)}, f32[320,640]{1,0:T(8,128)}, u32[]{:S(2)}, u32[]{:S(2)}) %collective-permute-start.9) | collective-permute-done | bytes 819232 | tf_op jit(solution)/shard_map/ppermute | solution.py:361
  111.2 8.6 %invert_first.3.swept_ref = f32[320,640]{1,0:T(8,128)S(1)} custom-call(s32[5]{0:T(128)S(1)} %stack.42.flags, f32[320,640]{1,0:T(8,128)} %collective-permute-done.9.own_ref), custom_call_target="tpu_custom_call" | custom-call | flops 9900000256 | bytes 31500000 | tf_op jit(solution)/shard_map/invert_first/pallas_call | solution.py:180
  119.9 0.0 collective-permute-done.12
  119.9 1.7 %add_add_fusion.loads_ref = f32[640,512]{1,0:T(8,128)S(1)} fusion(f32[640,512]{1,0:T(8,128)} %collective-permute-done.12, f32[640,512]{1,0:T(8,128)S(1)} %near_loads.1, f32[640,256]{1,0:T(8,128)S(1)} %copy-done.5, f32[640,256]{1,0:T(8,128)S(1)} %copy-done.3), kind=kLoop, calls=%fused_computation.1 | loop fusion | flops 983040 | bytes 5242880 | tf_op jit(solution)/shard_map/add | solution.py:451
  121.6 2.1 %collective-permute-start.13 = (f32[640,512]{1,0:T(8,128)S(1)}, f32[640,512]{1,0:T(8,128)S(1)}, u32[]{:S(2)}, u32[]{:S(2)}) collective-permute-start(f32[640,512]{1,0:T(8,128)S(1)} %add_add_fusion.loads_ref), channel_id=1, source_target_pairs={{0,8},{2,10},{4,12},{6,14},{8,16},{9,1},{10,18},{11,3},{12,20},{13... | collective-permute-start | bytes 3932168 | tf_op jit(solution)/shard_map/ppermute | solution.py:361
  123.7 1.6 collective-permute-done.10.square_ref.far_ref
  125.3 15.3 %invert_second.3.inverse_ref = f32[640,640]{1,0:T(8,128)S(1)} custom-call(s32[5]{0:T(128)S(1)} %stack.42.flags, f32[320,640]{1,0:T(8,128)} %collective-permute-done.9.own_ref, f32[320,640]{1,0:T(8,128)S(1)} %invert_first.3.swept_ref, f32[320,1024]{1,0:T(8,128)} %collective-permute-done.10.square_ref.far_ref), custom_call_target="tpu_custom_call" | custom-call | flops 15399999488 | bytes 49000000 | tf_op jit(solution)/shard_map/invert_second/pallas_call | solution.py:180
  140.6 8.3 %last_blocks.1 = (f32[640,640]{1,0:T(8,128)S(1)}, f32[320,640]{1,0:T(8,128)S(1)}, f32[320,640]{1,0:T(8,128)S(1)}) custom-call(s32[5]{0:T(128)S(1)} %stack.42.flags, f32[640,640]{1,0:T(8,128)S(1)} %invert_second.3.inverse_ref, f32[640,640]{1,0:T(8,128)S(1)} %copy-done.1, f32[320,1024]{1,0:T(8,128)} %collective-permute-done.10.square_ref.far_ref, ...), custom_call_target="tpu_custom_call" | custom-call | flops 6600000000 | bytes 21000000 | tf_op jit(solution)/shard_map/last_blocks/pallas_call | solution.py:180
  148.9 3.6 %collective-permute-start.11 = (f32[320,640]{1,0:T(8,128)S(1)}, f32[320,640]{1,0:T(8,128)S(1)}, u32[]{:S(2)}, u32[]{:S(2)}) collective-permute-start(f32[320,640]{1,0:T(8,128)S(1)} %get-tuple-element.30), channel_id=1, source_target_pairs={{0,1},{1,0},{2,3},{3,2},{4,5},{5,4},{6,7},{7,6},{8,9},{9,8},{10,11... | collective-permute-start | bytes 2457608 | tf_op jit(solution)/shard_map/ppermute | solution.py:361
  152.5 0.0 collective-permute-done.13.near_ref
  152.5 2.2 %last_loads.1 = (f32[640,256]{1,0:T(8,128)S(1)}, f32[640,256]{1,0:T(8,128)S(1)}) custom-call(s32[5]{0:T(128)S(1)} %stack.42.flags, f32[640,640]{1,0:T(8,128)S(1)} %get-tuple-element.31.g_ref, f32[640,512]{1,0:T(8,128)S(1)} %add_add_fusion.loads_ref, f32[640,512]{1,0:T(8,128)S(1)} %collective-permute-done.13.near_ref), custom_call_target="tpu_custom_call" | custom-call | flops 2200000000 | bytes 7000000 | tf_op jit(solution)/shard_map/last_loads/pallas_call | solution.py:180
  154.7 1.9 %collective-permute-start.14 = (f32[640,256]{1,0:T(8,128)S(1)}, f32[640,256]{1,0:T(8,128)S(1)}, u32[]{:S(2)}, u32[]{:S(2)}) collective-permute-start(f32[640,256]{1,0:T(8,128)S(1)} %get-tuple-element.35), channel_id=1, source_target_pairs={{0,1},{1,0},{2,3},{3,2},{4,5},{5,4},{6,7},{7,6},{8,9},{9,8},{10,11... | collective-permute-start | bytes 1966088 | tf_op jit(solution)/shard_map/ppermute | solution.py:361
  156.6 1.1 select_bitcast_fusion
  157.7 1.0 collective-permute-done.14
  158.7 0.9 add_bitcast_fusion
  (20 shorter events, 0.0 us)
Async XLA Ops:
  0.6 18.9 %copy-start.6 = (f32[1,160,640]{2,1,0:T(8,128)S(1)}, f32[1,160,640]{2,1,0:T(8,128)}, u32[]{:S(2)}) copy-start(f32[1,160,640]{2,1,0:T(8,128)} %param.4) | copy-start | bytes 1228804
  0.6 16.7 %copy-start.7 = (f32[1,640,256]{2,1,0:T(8,128)S(1)}, f32[1,640,256]{2,1,0:T(8,128)}, u32[]{:S(2)}) copy-start(f32[1,640,256]{2,1,0:T(8,128)} %param.7) | copy-start | bytes 1966084
  2.6 16.9 %collective-permute-start.3 = (f32[160,640]{1,0:T(8,128)S(1)}, f32[160,640]{1,0:T(8,128)}, u32[]{:S(2)}, u32[]{:S(2)}) collective-permute-start(f32[160,640]{1,0:T(8,128)S(1)} %fusion.4), channel_id=1, source_target_pairs={{0,8},{2,10},{4,12},{6,14},{8,16},{10,18},{12,20},{14,22},{16,24},... | collective-permute-start | bytes 1228808 | tf_op jit(solution)/shard_map/ppermute | solution.py:361
  4.1 15.5 %collective-permute-start.2 = (f32[160,640]{1,0:T(8,128)S(1)}, f32[160,640]{1,0:T(8,128)}, u32[]{:S(2)}, u32[]{:S(2)}) collective-permute-start(f32[160,640]{1,0:T(8,128)S(1)} %fusion.4), channel_id=1, source_target_pairs={{1,4},{3,6},{5,8},{4,1},{7,10},{6,3},{9,12},{8,5},{11,14},{10,7},{... | collective-permute-start | bytes 1228808 | tf_op jit(solution)/shard_map/ppermute | solution.py:361
  12.0 16.6 %collective-permute-start.1 = (f32[168,640]{1,0:T(8,128)S(1)}, f32[168,640]{1,0:T(8,128)}, u32[]{:S(2)}, u32[]{:S(2)}) collective-permute-start(f32[168,640]{1,0:T(8,128)S(1)} %maximum_maximum_fusion), channel_id=1, source_target_pairs={{0,4},{2,6},{4,8},{5,1},{6,10},{7,3},{8,12},{9,5},{10,14},{11,7},{... | collective-permute-start | bytes 1290248 | tf_op jit(solution)/shard_map/ppermute | solution.py:361
  14.1 12.4 %collective-permute-start = (f32[160,640]{1,0:T(8,128)S(1)}, f32[160,640]{1,0:T(8,128)S(1)}, u32[]{:S(2)}, u32[]{:S(2)}) collective-permute-start(f32[160,640]{1,0:T(8,128)S(1)} %fusion.4), channel_id=1, source_target_pairs={{1,8},{0,1},{3,10},{2,3},{5,12},{4,5},{7,14},{6,7},{9,16},{8,9},{1... | collective-permute-start | bytes 1228808 | tf_op jit(solution)/shard_map/ppermute | solution.py:361
  17.4 28.6 %collective-permute-start.7 = (f32[640,256]{1,0:T(8,128)S(1)}, f32[640,256]{1,0:T(8,128)S(1)}, u32[]{:S(2)}, u32[]{:S(2)}) collective-permute-start(f32[640,256]{1,0:T(8,128)S(1)} %bitcast.24), channel_id=1, source_target_pairs={{0,1},{1,0},{2,3},{3,2},{4,5},{5,4},{6,7},{7,6},{8,9},{9,8},{10,11... | collective-permute-start | bytes 1966088 | tf_op jit(solution)/shard_map/ppermute | solution.py:361
  31.1 19.9 %collective-permute-start.4 = (f32[320,320]{1,0:T(8,128)S(1)}, f32[320,320]{1,0:T(8,128)S(1)}, u32[]{:S(2)}, u32[]{:S(2)}) collective-permute-start(f32[320,320]{1,0:T(8,128)S(1)} %slice_select_fusion), channel_id=1, source_target_pairs={{0,2},{1,3},{2,0},{3,1},{4,6},{5,7},{6,4},{7,5},{8,10},{9,11},{10,... | collective-permute-start | bytes 1228808 | tf_op jit(solution)/shard_map/ppermute | solution.py:361
  42.9 27.5 %collective-permute-start.5 = (f32[320,320]{1,0:T(8,128)S(1)}, f32[320,320]{1,0:T(8,128)S(1)}, u32[]{:S(2)}, u32[]{:S(2)}) collective-permute-start(f32[320,320]{1,0:T(8,128)S(1)} %fusion.1), channel_id=1, source_target_pairs={{0,2},{1,3},{2,0},{3,1},{4,6},{5,7},{6,4},{7,5},{8,10},{9,11},{10,... | collective-permute-start | bytes 1228808 | tf_op jit(solution)/shard_map/ppermute | solution.py:361
  46.1 0.9 copy-start.2
  46.1 1.0 copy-start.4
  47.1 42.2 %collective-permute-start.8 = (f32[640,512]{1,0:T(8,128)S(1)}, f32[640,512]{1,0:T(8,128)S(1)}, u32[]{:S(2)}, u32[]{:S(2)}) collective-permute-start(f32[640,512]{1,0:T(8,128)S(1)} %pad_maximum_fusion), channel_id=1, source_target_pairs={{0,4},{2,6},{4,8},{5,1},{6,10},{7,3},{8,12},{9,5},{10,14},{11,7},{... | collective-permute-start | bytes 3932168 | tf_op jit(solution)/shard_map/ppermute | solution.py:361
  70.4 18.6 %copy-start.8 = (f32[1,640]{1,0:T(1,128)S(1)}, f32[1,640]{1,0:T(1,128)}, u32[]{:S(2)}) copy-start(f32[1,640]{1,0:T(1,128)} %param.6) | copy-start | bytes 7684
  80.3 13.2 %collective-permute-start.6 = (f32[320,1024]{1,0:T(8,128)S(1)}, f32[320,1024]{1,0:T(8,128)S(1)}, u32[]{:S(2)}, u32[]{:S(2)}) collective-permute-start(f32[320,1024]{1,0:T(8,128)S(1)} %get-tuple-element.21.rest_ref), channel_id=1, source_target_pairs={{0,1},{1,0},{2,3},{3,2},{4,5},{5,4},{6,7},{7,6},{8,9},{9,8},{10,11... | collective-permute-start | bytes 3932168 | tf_op jit(solution)/shard_map/ppermute | solution.py:361
  93.5 1.2 copy-start
  94.7 16.5 %collective-permute-start.9 = (f32[320,640]{1,0:T(8,128)S(1)}, f32[320,640]{1,0:T(8,128)}, u32[]{:S(2)}, u32[]{:S(2)}) collective-permute-start(f32[320,640]{1,0:T(8,128)S(1)} %get-tuple-element.26.diag_ref), channel_id=1, source_target_pairs={{0,8},{2,10},{4,12},{6,14},{8,16},{9,1},{10,18},{11,3},{12,20},{13... | collective-permute-start | bytes 2457608 | tf_op jit(solution)/shard_map/ppermute | solution.py:361
  98.7 21.1 %collective-permute-start.12 = (f32[640,512]{1,0:T(8,128)S(1)}, f32[640,512]{1,0:T(8,128)}, u32[]{:S(2)}, u32[]{:S(2)}) collective-permute-start(f32[640,512]{1,0:T(8,128)S(1)} %near_loads.1), channel_id=1, source_target_pairs={{0,1},{1,0},{2,3},{3,2},{4,5},{5,4},{6,7},{7,6},{8,9},{9,8},{10,11... | collective-permute-start | bytes 3932168 | tf_op jit(solution)/shard_map/ppermute | solution.py:361
  102.7 22.6 %collective-permute-start.10 = (f32[320,1024]{1,0:T(8,128)S(1)}, f32[320,1024]{1,0:T(8,128)}, u32[]{:S(2)}, u32[]{:S(2)}) collective-permute-start(f32[320,1024]{1,0:T(8,128)S(1)} %get-tuple-element.27), channel_id=1, source_target_pairs={{0,8},{2,10},{4,12},{6,14},{8,16},{9,1},{10,18},{11,3},{12,20},{13... | collective-permute-start | bytes 3932168 | tf_op jit(solution)/shard_map/ppermute | solution.py:361
  105.0 14.9 %copy-start.3 = (f32[640,256]{1,0:T(8,128)S(1)}, f32[640,256]{1,0:T(8,128)}, u32[]{:S(2)}) copy-start(f32[640,256]{1,0:T(8,128)} %copy-done.2) | copy-start | bytes 1966084
  105.0 14.9 %copy-start.5 = (f32[640,256]{1,0:T(8,128)S(1)}, f32[640,256]{1,0:T(8,128)}, u32[]{:S(2)}) copy-start(f32[640,256]{1,0:T(8,128)} %copy-done.4) | copy-start | bytes 1966084
  121.6 19.0 %copy-start.1 = (f32[640,640]{1,0:T(8,128)S(1)}, f32[640,640]{1,0:T(8,128)}, u32[]{:S(2)}) copy-start(f32[640,640]{1,0:T(8,128)} %copy-done) | copy-start | bytes 4915204
  121.6 30.9 %collective-permute-start.13 = (f32[640,512]{1,0:T(8,128)S(1)}, f32[640,512]{1,0:T(8,128)S(1)}, u32[]{:S(2)}, u32[]{:S(2)}) collective-permute-start(f32[640,512]{1,0:T(8,128)S(1)} %add_add_fusion.loads_ref), channel_id=1, source_target_pairs={{0,8},{2,10},{4,12},{6,14},{8,16},{9,1},{10,18},{11,3},{12,20},{13... | collective-permute-start | bytes 3932168 | tf_op jit(solution)/shard_map/ppermute | solution.py:361
  148.9 7.7 %collective-permute-start.11 = (f32[320,640]{1,0:T(8,128)S(1)}, f32[320,640]{1,0:T(8,128)S(1)}, u32[]{:S(2)}, u32[]{:S(2)}) collective-permute-start(f32[320,640]{1,0:T(8,128)S(1)} %get-tuple-element.30), channel_id=1, source_target_pairs={{0,1},{1,0},{2,3},{3,2},{4,5},{5,4},{6,7},{7,6},{8,9},{9,8},{10,11... | collective-permute-start | bytes 2457608 | tf_op jit(solution)/shard_map/ppermute | solution.py:361
  154.7 4.0 %collective-permute-start.14 = (f32[640,256]{1,0:T(8,128)S(1)}, f32[640,256]{1,0:T(8,128)S(1)}, u32[]{:S(2)}, u32[]{:S(2)}) collective-permute-start(f32[640,256]{1,0:T(8,128)S(1)} %get-tuple-element.35), channel_id=1, source_target_pairs={{0,1},{1,0},{2,3},{3,2},{4,5},{5,4},{6,7},{7,6},{8,9},{9,8},{10,11... | collective-permute-start | bytes 1966088 | tf_op jit(solution)/shard_map/ppermute | solution.py:361
where the time goes:
time: 160 us
  Pallas kernels  73.8 us (46%)
  starting transfers between devices  50.7 us (32%)
  waiting for transfers between devices  21.8 us (14%)
  other arithmetic  10.5 us (7%)
  local copies, waits for them, and re-layouts  1.75 us (1%)
    pallas_call x10, Pallas kernels, local_call(): pl.pallas_call(body, out_shape=[jax.ShapeDtypeStruct(shape, jnp.float32)...  73.8 us
    ppermute x15, starting transfers between devices, move(): return lax.ppermute(array, AXES, pairs_of(layers, moves))  50.7 us
    ppermute x15, waiting for transfers between devices, move(): return lax.ppermute(array, AXES, pairs_of(layers, moves))  21.8 us
  transfers between devices with their start and end apart: 15, of which 6 were waited for; matrix products, arithmetic and copies ran while one was open for 5% of the time, Pallas kernels for 46%

commit v1 on v0

--- a/solution.py
+++ b/solution.py
@@ -372,6 +372,12 @@
     def opposite(array):
         return move(array, (0, 0, 1, 0), (1, 0, 1, 1))
 
+    def flipped(array):
+        pairs = pairs_of(layers, [(1, 1, 1, 0), (0, -1, 1, 1)])
+        for side in range(2):
+            pairs.append((device(layers - 1, side, 1), device(layers - 1, 1 - side, 1)))
+        return lax.ppermute(array, AXES, pairs)
+
     def pick(on_upper, on_lower):
         return jnp.where(upper, on_upper, on_lower)
 
@@ -420,7 +426,7 @@
     loads_in = sibling(loads_0)
     loads_0 = jnp.concatenate([pick(loads_in, loads_0), pick(loads_0, loads_in)], axis=1)
     (swept_0,) = local_call(first_kernel, "invert_first", 9, flags_0, [d_own], [own_shape])
-    x_square = opposite(after(square(x_own, half), swept_0))
+    x_square = flipped(after(square(x_own, half), swept_0))
     near_loads = straight(after(loads_0, swept_0), 1)
     (inverse,) = local_call(
         functools.partial(second_kernel, 0), "invert_second", 14, flags_0,

time: 160 us -> 154 us (0.963)
  waiting for transfers between devices: 21.8 us -> 16 us
    ppermute x15 -> x14, waiting for transfers between devices: 21.8 us -> 16 us  [move(): return lax.ppermute(array, AXES, pairs_of(layers, moves))]
    ppermute x15 -> x14, starting transfers between devices: 50.7 us -> 45.3 us  [move(): return lax.ppermute(array, AXES, pairs_of(layers, moves))]
    ppermute x0 -> x1, starting transfers between devices: none -> 4.84 us  [flipped(): return lax.ppermute(array, AXES, pairs)]
  transfers between devices with their start and end apart: 15 -> 15, of which waited for: 6 -> 5; matrix products, arithmetic and copies ran while one was open for 5% -> 5% of each run, Pallas kernels for 46% -> 48%
where the time goes in v1:
time: 154 us; the launch traced here: 153 us
  Pallas kernels  73.8 us (48%)
  starting transfers between devices  50.1 us (33%)
  waiting for transfers between devices  16 us (10%)
  other arithmetic  10.5 us (7%)
  local copies, waits for them, and re-layouts  1.75 us (1%)
    pallas_call x10, Pallas kernels, local_call(): pl.pallas_call(body, out_shape=[jax.ShapeDtypeStruct(shape, jnp.float32)...  73.8 us
    ppermute x14, starting transfers between devices, move(): return lax.ppermute(array, AXES, pairs_of(layers, moves))  45.3 us
    ppermute x14, waiting for transfers between devices, move(): return lax.ppermute(array, AXES, pairs_of(layers, moves))  16 us
    ppermute x1, starting transfers between devices, flipped(): return lax.ppermute(array, AXES, pairs)  4.84 us
  transfers between devices with their start and end apart: 15, of which 5 were waited for; matrix products, arithmetic and copies ran while one was open for 5% of the time, Pallas kernels for 48%

profile of v1, /device:TPU:251, one launch (start us, length us, event | category | flops | bytes accessed | tf_op | source)
XLA Modules:
  0.0 153.2 jit_solution(9360508274070790428)
XLA Ops:
  0.6 0.0 copy-start.6
  0.7 0.8 multiply_add_fusion
  1.4 0.1 constant_dynamic-slice_fusion
  1.5 1.1 fusion.4
  2.6 1.4 collective-permute-start.3
  4.1 7.0 %collective-permute-start.2 = (f32[160,640]{1,0:T(8,128)S(1)}, f32[160,640]{1,0:T(8,128)}, u32[]{:S(2)}, u32[]{:S(2)}) collective-permute-start(f32[160,640]{1,0:T(8,128)S(1)} %fusion.4), channel_id=1, source_target_pairs={{1,4},{3,6},{5,8},{4,1},{7,10},{6,3},{9,12},{8,5},{11,14},{10,7},{... | collective-permute-start | bytes 1228808 | tf_op jit(solution)/shard_map/ppermute | solution.py:361
  11.1 0.1 pad.11.clone
  11.2 0.8 maximum_maximum_fusion
  12.0 2.1 %collective-permute-start.1 = (f32[168,640]{1,0:T(8,128)S(1)}, f32[168,640]{1,0:T(8,128)}, u32[]{:S(2)}, u32[]{:S(2)}) collective-permute-start(f32[168,640]{1,0:T(8,128)S(1)} %maximum_maximum_fusion), channel_id=1, source_target_pairs={{0,4},{2,6},{4,8},{5,1},{6,10},{7,3},{8,12},{9,5},{10,14},{11,7},{... | collective-permute-start | bytes 1290248 | tf_op jit(solution)/shard_map/ppermute | solution.py:361
  14.1 3.3 %collective-permute-start = (f32[160,640]{1,0:T(8,128)S(1)}, f32[160,640]{1,0:T(8,128)S(1)}, u32[]{:S(2)}, u32[]{:S(2)}) collective-permute-start(f32[160,640]{1,0:T(8,128)S(1)} %fusion.4), channel_id=1, source_target_pairs={{1,8},{0,1},{3,10},{2,3},{5,12},{4,5},{7,14},{6,7},{9,16},{8,9},{1... | collective-permute-start | bytes 1228808 | tf_op jit(solution)/shard_map/ppermute | solution.py:361
  17.4 1.9 %collective-permute-start.7 = (f32[640,256]{1,0:T(8,128)S(1)}, f32[640,256]{1,0:T(8,128)S(1)}, u32[]{:S(2)}, u32[]{:S(2)}) collective-permute-start(f32[640,256]{1,0:T(8,128)S(1)} %bitcast.24), channel_id=1, source_target_pairs={{0,1},{1,0},{2,3},{3,2},{4,5},{5,4},{6,7},{7,6},{8,9},{9,8},{10,11... | collective-permute-start | bytes 1966088 | tf_op jit(solution)/shard_map/ppermute | solution.py:361
  19.4 0.1 pad.4.clone
  19.4 0.1 stack.43.flags
  19.5 0.0 collective-permute-done.3
  19.5 0.0 collective-permute-done.2
  19.5 1.1 broadcast_select_fusion.3
  20.7 5.8 %collective-permute-done = f32[160,640]{1,0:T(8,128)S(1)} collective-permute-done((f32[160,640]{1,0:T(8,128)S(1)}, f32[160,640]{1,0:T(8,128)S(1)}, u32[]{:S(2)}, u32[]{:S(2)}) %collective-permute-start) | collective-permute-done | bytes 409632 | tf_op jit(solution)/shard_map/ppermute | solution.py:361
  26.5 2.1 %collective-permute-done.1 = f32[168,640]{1,0:T(8,128)} collective-permute-done((f32[168,640]{1,0:T(8,128)S(1)}, f32[168,640]{1,0:T(8,128)}, u32[]{:S(2)}, u32[]{:S(2)}) %collective-permute-start.1) | collective-permute-done | bytes 430112 | tf_op jit(solution)/shard_map/ppermute | solution.py:361
  28.6 1.1 slice_select_fusion.2
  29.7 0.2 fusion.1
  29.9 0.8 fusion.7
  30.7 0.2 pad_maximum_fusion.2
  30.9 0.2 slice_select_fusion
  31.1 3.8 %collective-permute-start.4 = (f32[320,320]{1,0:T(8,128)S(1)}, f32[320,320]{1,0:T(8,128)S(1)}, u32[]{:S(2)}, u32[]{:S(2)}) collective-permute-start(f32[320,320]{1,0:T(8,128)S(1)} %slice_select_fusion), channel_id=1, source_target_pairs={{0,2},{1,3},{2,0},{3,1},{4,6},{5,7},{6,4},{7,5},{8,10},{9,11},{10,... | collective-permute-start | bytes 1228808 | tf_op jit(solution)/shard_map/ppermute | solution.py:361
  34.9 8.0 %invert_first.2.swept_ref = f32[320,640]{1,0:T(8,128)S(1)} custom-call(s32[5]{0:T(128)S(1)} %stack.43.flags, f32[320,640]{1,0:T(8,128)S(1)} %get-tuple-element.46.own_ref), custom_call_target="tpu_custom_call" | custom-call | flops 9900000256 | bytes 31500000 | tf_op jit(solution)/shard_map/invert_first/pallas_call | solution.py:180
  42.9 4.8 %collective-permute-start.5 = (f32[320,320]{1,0:T(8,128)S(1)}, f32[320,320]{1,0:T(8,128)S(1)}, u32[]{:S(2)}, u32[]{:S(2)}) collective-permute-start(f32[320,320]{1,0:T(8,128)S(1)} %fusion.1), channel_id=1, source_target_pairs={{1,6},{3,4},{5,10},{4,3},{7,8},{6,1},{9,14},{8,7},{11,12},{10,5},{... | collective-permute-start | bytes 1228808 | tf_op jit(solution)/shard_map/ppermute | solution.py:379
  47.8 0.0 collective-permute-done.7
  47.8 0.1 broadcast_select_fusion.1
  47.9 0.0 copy-start.4
  47.9 0.1 pad_maximum_fusion
  48.1 0.7 copy-done.2
  48.7 0.2 copy-done.4
  48.9 3.5 %collective-permute-start.8 = (f32[640,512]{1,0:T(8,128)S(1)}, f32[640,512]{1,0:T(8,128)S(1)}, u32[]{:S(2)}, u32[]{:S(2)}) collective-permute-start(f32[640,512]{1,0:T(8,128)S(1)} %pad_maximum_fusion), channel_id=1, source_target_pairs={{0,4},{2,6},{4,8},{5,1},{6,10},{7,3},{8,12},{9,5},{10,14},{11,7},{... | collective-permute-start | bytes 3932168 | tf_op jit(solution)/shard_map/ppermute | solution.py:361
  52.5 14.3 %invert_second.2.inverse_ref = f32[640,640]{1,0:T(8,128)S(1)} custom-call(s32[5]{0:T(128)S(1)} %stack.43.flags, f32[320,640]{1,0:T(8,128)S(1)} %get-tuple-element.46.own_ref, f32[320,640]{1,0:T(8,128)S(1)} %invert_first.2.swept_ref, f32[320,320]{1,0:T(8,128)S(1)} %collective-permute-done.4.square_ref), custom_call_target="tpu_custom_call" | custom-call | flops 15399999488 | bytes 49000000 | tf_op jit(solution)/shard_map/invert_second/pallas_call | solution.py:180
  66.8 0.0 collective-permute-done.5.square_ref
  66.8 0.0 copy-start.8
  66.8 9.9 %rest.1 = (f32[640,640]{1,0:T(8,128)S(1)}, f32[320,1024]{1,0:T(8,128)S(1)}) custom-call(s32[5]{0:T(128)S(1)} %stack.43.flags, f32[640,640]{1,0:T(8,128)S(1)} %invert_second.2.inverse_ref, f32[320,640]{1,0:T(8,128)S(1)} %get-tuple-element.47.x_ref, f32[320,320]{1,0:T(8,128)S(1)} %collective-permute-done.5.square_ref), custom_call_target="tpu_custom_call" | custom-call | flops 1100000000 | bytes 3500000 | tf_op jit(solution)/shard_map/rest/pallas_call | solution.py:180
  76.8 4.2 %collective-permute-start.6 = (f32[320,1024]{1,0:T(8,128)S(1)}, f32[320,1024]{1,0:T(8,128)S(1)}, u32[]{:S(2)}, u32[]{:S(2)}) collective-permute-start(f32[320,1024]{1,0:T(8,128)S(1)} %get-tuple-element.21.rest_ref), channel_id=1, source_target_pairs={{0,1},{1,0},{2,3},{3,2},{4,5},{5,4},{6,7},{7,6},{8,9},{9,8},{10,11... | collective-permute-start | bytes 3932168 | tf_op jit(solution)/shard_map/ppermute | solution.py:361
  81.0 0.1 broadcast_select_fusion.5
  81.1 0.1 fusion.5
  81.2 0.1 select_subtract_fusion.y_square_ref
  81.3 4.2 %links.1 = (f32[640,640]{1,0:T(8,128)S(1)}, f32[320,640]{1,0:T(8,128)S(1)}) custom-call(s32[5]{0:T(128)S(1)} %stack.43.flags, f32[640,640]{1,0:T(8,128)S(1)} %get-tuple-element.32.g_ref, f32[320,640]{1,0:T(8,128)S(1)} %get-tuple-element.24.y_ref, f32[320,320]{1,0:T(8,128)S(1)} %select_subtract_fusion.y_square_ref), custom_call_target="tpu_custom_call" | custom-call | flops 5500000256 | bytes 17500000 | tf_op jit(solution)/shard_map/links/pallas_call | solution.py:180
  85.5 0.0 collective-permute-done.6.came_ref
  85.5 0.7 combine.1
  86.3 0.4 copy-done
  86.7 1.9 %collective-permute-start.9 = (f32[320,640]{1,0:T(8,128)S(1)}, f32[320,640]{1,0:T(8,128)}, u32[]{:S(2)}, u32[]{:S(2)}) collective-permute-start(f32[320,640]{1,0:T(8,128)S(1)} %get-tuple-element.26.diag_ref), channel_id=1, source_target_pairs={{0,8},{2,10},{4,12},{6,14},{8,16},{9,1},{10,18},{11,3},{12,20},{13... | collective-permute-start | bytes 2457608 | tf_op jit(solution)/shard_map/ppermute | solution.py:361
  88.6 2.1 %near_loads.1 = f32[640,512]{1,0:T(8,128)S(1)} custom-call(s32[5]{0:T(128)S(1)} %stack.43.flags, f32[640,640]{1,0:T(8,128)S(1)} %get-tuple-element.32.g_ref, f32[640,512]{1,0:T(8,128)S(1)} %collective-permute-done.8.loads_ref), custom_call_target="tpu_custom_call" | custom-call | flops 2200000000 | bytes 7000000 | tf_op jit(solution)/shard_map/near_loads/pallas_call | solution.py:180
  90.7 5.6 %collective-permute-start.12 = (f32[640,512]{1,0:T(8,128)S(1)}, f32[640,512]{1,0:T(8,128)}, u32[]{:S(2)}, u32[]{:S(2)}) collective-permute-start(f32[640,512]{1,0:T(8,128)S(1)} %near_loads.1), channel_id=1, source_target_pairs={{0,1},{1,0},{2,3},{3,2},{4,5},{5,4},{6,7},{7,6},{8,9},{9,8},{10,11... | collective-permute-start | bytes 3932168 | tf_op jit(solution)/shard_map/ppermute | solution.py:361
  96.3 2.1 %collective-permute-start.10 = (f32[320,1024]{1,0:T(8,128)S(1)}, f32[320,1024]{1,0:T(8,128)}, u32[]{:S(2)}, u32[]{:S(2)}) collective-permute-start(f32[320,1024]{1,0:T(8,128)S(1)} %get-tuple-element.27), channel_id=1, source_target_pairs={{0,8},{2,10},{4,12},{6,14},{8,16},{9,1},{10,18},{11,3},{12,20},{13... | collective-permute-start | bytes 3932168 | tf_op jit(solution)/shard_map/ppermute | solution.py:361
  98.5 0.1 stack.42.flags
  98.6 4.6 %collective-permute-done.9.own_ref = f32[320,640]{1,0:T(8,128)} collective-permute-done((f32[320,640]{1,0:T(8,128)S(1)}, f32[320,640]{1,0:T(8,128)}, u32[]{:S(2)}, u32[]{:S(2)}) %collective-permute-start.9) | collective-permute-done | bytes 819232 | tf_op jit(solution)/shard_map/ppermute | solution.py:361
  103.2 8.6 %invert_first.3.swept_ref = f32[320,640]{1,0:T(8,128)S(1)} custom-call(s32[5]{0:T(128)S(1)} %stack.42.flags, f32[320,640]{1,0:T(8,128)} %collective-permute-done.9.own_ref), custom_call_target="tpu_custom_call" | custom-call | flops 9900000256 | bytes 31500000 | tf_op jit(solution)/shard_map/invert_first/pallas_call | solution.py:180
  111.9 0.0 collective-permute-done.12
  111.9 1.7 %add_add_fusion.loads_ref = f32[640,512]{1,0:T(8,128)S(1)} fusion(f32[640,512]{1,0:T(8,128)} %collective-permute-done.12, f32[640,512]{1,0:T(8,128)S(1)} %near_loads.1, f32[640,256]{1,0:T(8,128)S(1)} %copy-done.5, f32[640,256]{1,0:T(8,128)S(1)} %copy-done.3), kind=kLoop, calls=%fused_computation.1 | loop fusion | flops 983040 | bytes 5242880 | tf_op jit(solution)/shard_map/add | solution.py:457
  113.6 2.1 %collective-permute-start.13 = (f32[640,512]{1,0:T(8,128)S(1)}, f32[640,512]{1,0:T(8,128)S(1)}, u32[]{:S(2)}, u32[]{:S(2)}) collective-permute-start(f32[640,512]{1,0:T(8,128)S(1)} %add_add_fusion.loads_ref), channel_id=1, source_target_pairs={{0,8},{2,10},{4,12},{6,14},{8,16},{9,1},{10,18},{11,3},{12,20},{13... | collective-permute-start | bytes 3932168 | tf_op jit(solution)/shard_map/ppermute | solution.py:361
  115.7 2.4 %collective-permute-done.10.square_ref.far_ref = f32[320,1024]{1,0:T(8,128)} collective-permute-done((f32[320,1024]{1,0:T(8,128)S(1)}, f32[320,1024]{1,0:T(8,128)}, u32[]{:S(2)}, u32[]{:S(2)}) %collective-permute-start.10) | collective-permute-done | bytes 1310752 | tf_op jit(solution)/shard_map/ppermute | solution.py:361
  118.1 15.4 %invert_second.3.inverse_ref = f32[640,640]{1,0:T(8,128)S(1)} custom-call(s32[5]{0:T(128)S(1)} %stack.42.flags, f32[320,640]{1,0:T(8,128)} %collective-permute-done.9.own_ref, f32[320,640]{1,0:T(8,128)S(1)} %invert_first.3.swept_ref, f32[320,1024]{1,0:T(8,128)} %collective-permute-done.10.square_ref.far_ref), custom_call_target="tpu_custom_call" | custom-call | flops 15399999488 | bytes 49000000 | tf_op jit(solution)/shard_map/invert_second/pallas_call | solution.py:180
  133.5 8.3 %last_blocks.1 = (f32[640,640]{1,0:T(8,128)S(1)}, f32[320,640]{1,0:T(8,128)S(1)}, f32[320,640]{1,0:T(8,128)S(1)}) custom-call(s32[5]{0:T(128)S(1)} %stack.42.flags, f32[640,640]{1,0:T(8,128)S(1)} %invert_second.3.inverse_ref, f32[640,640]{1,0:T(8,128)S(1)} %copy-done.1, f32[320,1024]{1,0:T(8,128)} %collective-permute-done.10.square_ref.far_ref, ...), custom_call_target="tpu_custom_call" | custom-call | flops 6600000000 | bytes 21000000 | tf_op jit(solution)/shard_map/last_blocks/pallas_call | solution.py:180
  141.8 4.3 %collective-permute-start.11 = (f32[320,640]{1,0:T(8,128)S(1)}, f32[320,640]{1,0:T(8,128)S(1)}, u32[]{:S(2)}, u32[]{:S(2)}) collective-permute-start(f32[320,640]{1,0:T(8,128)S(1)} %get-tuple-element.30), channel_id=1, source_target_pairs={{0,1},{1,0},{2,3},{3,2},{4,5},{5,4},{6,7},{7,6},{8,9},{9,8},{10,11... | collective-permute-start | bytes 2457608 | tf_op jit(solution)/shard_map/ppermute | solution.py:361
  146.1 2.2 %last_loads.1 = (f32[640,256]{1,0:T(8,128)S(1)}, f32[640,256]{1,0:T(8,128)S(1)}) custom-call(s32[5]{0:T(128)S(1)} %stack.42.flags, f32[640,640]{1,0:T(8,128)S(1)} %get-tuple-element.31.g_ref, f32[640,512]{1,0:T(8,128)S(1)} %add_add_fusion.loads_ref, f32[640,512]{1,0:T(8,128)S(1)} %collective-permute-done.13.near_ref), custom_call_target="tpu_custom_call" | custom-call | flops 2200000000 | bytes 7000000 | tf_op jit(solution)/shard_map/last_loads/pallas_call | solution.py:180
  148.3 1.9 %collective-permute-start.14 = (f32[640,256]{1,0:T(8,128)S(1)}, f32[640,256]{1,0:T(8,128)S(1)}, u32[]{:S(2)}, u32[]{:S(2)}) collective-permute-start(f32[640,256]{1,0:T(8,128)S(1)} %get-tuple-element.35), channel_id=1, source_target_pairs={{0,1},{1,0},{2,3},{3,2},{4,5},{5,4},{6,7},{7,6},{8,9},{9,8},{10,11... | collective-permute-start | bytes 1966088 | tf_op jit(solution)/shard_map/ppermute | solution.py:361
  150.3 1.1 select_bitcast_fusion
  151.4 1.0 collective-permute-done.14
  152.3 0.9 add_bitcast_fusion
  (20 shorter events, 0.1 us)
Async XLA Ops:
  0.6 18.9 %copy-start.6 = (f32[1,160,640]{2,1,0:T(8,128)S(1)}, f32[1,160,640]{2,1,0:T(8,128)}, u32[]{:S(2)}) copy-start(f32[1,160,640]{2,1,0:T(8,128)} %param.4) | copy-start | bytes 1228804
  0.6 16.7 %copy-start.7 = (f32[1,640,256]{2,1,0:T(8,128)S(1)}, f32[1,640,256]{2,1,0:T(8,128)}, u32[]{:S(2)}) copy-start(f32[1,640,256]{2,1,0:T(8,128)} %param.7) | copy-start | bytes 1966084
  2.6 16.9 %collective-permute-start.3 = (f32[160,640]{1,0:T(8,128)S(1)}, f32[160,640]{1,0:T(8,128)}, u32[]{:S(2)}, u32[]{:S(2)}) collective-permute-start(f32[160,640]{1,0:T(8,128)S(1)} %fusion.4), channel_id=1, source_target_pairs={{0,8},{2,10},{4,12},{6,14},{8,16},{10,18},{12,20},{14,22},{16,24},... | collective-permute-start | bytes 1228808 | tf_op jit(solution)/shard_map/ppermute | solution.py:361
  4.1 15.5 %collective-permute-start.2 = (f32[160,640]{1,0:T(8,128)S(1)}, f32[160,640]{1,0:T(8,128)}, u32[]{:S(2)}, u32[]{:S(2)}) collective-permute-start(f32[160,640]{1,0:T(8,128)S(1)} %fusion.4), channel_id=1, source_target_pairs={{1,4},{3,6},{5,8},{4,1},{7,10},{6,3},{9,12},{8,5},{11,14},{10,7},{... | collective-permute-start | bytes 1228808 | tf_op jit(solution)/shard_map/ppermute | solution.py:361
  12.0 16.6 %collective-permute-start.1 = (f32[168,640]{1,0:T(8,128)S(1)}, f32[168,640]{1,0:T(8,128)}, u32[]{:S(2)}, u32[]{:S(2)}) collective-permute-start(f32[168,640]{1,0:T(8,128)S(1)} %maximum_maximum_fusion), channel_id=1, source_target_pairs={{0,4},{2,6},{4,8},{5,1},{6,10},{7,3},{8,12},{9,5},{10,14},{11,7},{... | collective-permute-start | bytes 1290248 | tf_op jit(solution)/shard_map/ppermute | solution.py:361
  14.1 12.4 %collective-permute-start = (f32[160,640]{1,0:T(8,128)S(1)}, f32[160,640]{1,0:T(8,128)S(1)}, u32[]{:S(2)}, u32[]{:S(2)}) collective-permute-start(f32[160,640]{1,0:T(8,128)S(1)} %fusion.4), channel_id=1, source_target_pairs={{1,8},{0,1},{3,10},{2,3},{5,12},{4,5},{7,14},{6,7},{9,16},{8,9},{1... | collective-permute-start | bytes 1228808 | tf_op jit(solution)/shard_map/ppermute | solution.py:361
  17.4 30.4 %collective-permute-start.7 = (f32[640,256]{1,0:T(8,128)S(1)}, f32[640,256]{1,0:T(8,128)S(1)}, u32[]{:S(2)}, u32[]{:S(2)}) collective-permute-start(f32[640,256]{1,0:T(8,128)S(1)} %bitcast.24), channel_id=1, source_target_pairs={{0,1},{1,0},{2,3},{3,2},{4,5},{5,4},{6,7},{7,6},{8,9},{9,8},{10,11... | collective-permute-start | bytes 1966088 | tf_op jit(solution)/shard_map/ppermute | solution.py:361
  31.1 21.4 %collective-permute-start.4 = (f32[320,320]{1,0:T(8,128)S(1)}, f32[320,320]{1,0:T(8,128)S(1)}, u32[]{:S(2)}, u32[]{:S(2)}) collective-permute-start(f32[320,320]{1,0:T(8,128)S(1)} %slice_select_fusion), channel_id=1, source_target_pairs={{0,2},{1,3},{2,0},{3,1},{4,6},{5,7},{6,4},{7,5},{8,10},{9,11},{10,... | collective-permute-start | bytes 1228808 | tf_op jit(solution)/shard_map/ppermute | solution.py:361
  42.9 23.9 %collective-permute-start.5 = (f32[320,320]{1,0:T(8,128)S(1)}, f32[320,320]{1,0:T(8,128)S(1)}, u32[]{:S(2)}, u32[]{:S(2)}) collective-permute-start(f32[320,320]{1,0:T(8,128)S(1)} %fusion.1), channel_id=1, source_target_pairs={{1,6},{3,4},{5,10},{4,3},{7,8},{6,1},{9,14},{8,7},{11,12},{10,5},{... | collective-permute-start | bytes 1228808 | tf_op jit(solution)/shard_map/ppermute | solution.py:379
  47.9 0.9 copy-start.2
  47.9 1.0 copy-start.4
  48.9 32.3 %collective-permute-start.8 = (f32[640,512]{1,0:T(8,128)S(1)}, f32[640,512]{1,0:T(8,128)S(1)}, u32[]{:S(2)}, u32[]{:S(2)}) collective-permute-start(f32[640,512]{1,0:T(8,128)S(1)} %pad_maximum_fusion), channel_id=1, source_target_pairs={{0,4},{2,6},{4,8},{5,1},{6,10},{7,3},{8,12},{9,5},{10,14},{11,7},{... | collective-permute-start | bytes 3932168 | tf_op jit(solution)/shard_map/ppermute | solution.py:361
  66.8 14.2 %copy-start.8 = (f32[1,640]{1,0:T(1,128)S(1)}, f32[1,640]{1,0:T(1,128)}, u32[]{:S(2)}) copy-start(f32[1,640]{1,0:T(1,128)} %param.6) | copy-start | bytes 7684
  76.8 8.8 %collective-permute-start.6 = (f32[320,1024]{1,0:T(8,128)S(1)}, f32[320,1024]{1,0:T(8,128)S(1)}, u32[]{:S(2)}, u32[]{:S(2)}) collective-permute-start(f32[320,1024]{1,0:T(8,128)S(1)} %get-tuple-element.21.rest_ref), channel_id=1, source_target_pairs={{0,1},{1,0},{2,3},{3,2},{4,5},{5,4},{6,7},{7,6},{8,9},{9,8},{10,11... | collective-permute-start | bytes 3932168 | tf_op jit(solution)/shard_map/ppermute | solution.py:361
  85.5 1.2 copy-start
  86.7 16.5 %collective-permute-start.9 = (f32[320,640]{1,0:T(8,128)S(1)}, f32[320,640]{1,0:T(8,128)}, u32[]{:S(2)}, u32[]{:S(2)}) collective-permute-start(f32[320,640]{1,0:T(8,128)S(1)} %get-tuple-element.26.diag_ref), channel_id=1, source_target_pairs={{0,8},{2,10},{4,12},{6,14},{8,16},{9,1},{10,18},{11,3},{12,20},{13... | collective-permute-start | bytes 2457608 | tf_op jit(solution)/shard_map/ppermute | solution.py:361
  90.7 21.1 %collective-permute-start.12 = (f32[640,512]{1,0:T(8,128)S(1)}, f32[640,512]{1,0:T(8,128)}, u32[]{:S(2)}, u32[]{:S(2)}) collective-permute-start(f32[640,512]{1,0:T(8,128)S(1)} %near_loads.1), channel_id=1, source_target_pairs={{0,1},{1,0},{2,3},{3,2},{4,5},{5,4},{6,7},{7,6},{8,9},{9,8},{10,11... | collective-permute-start | bytes 3932168 | tf_op jit(solution)/shard_map/ppermute | solution.py:361
  96.3 21.8 %collective-permute-start.10 = (f32[320,1024]{1,0:T(8,128)S(1)}, f32[320,1024]{1,0:T(8,128)}, u32[]{:S(2)}, u32[]{:S(2)}) collective-permute-start(f32[320,1024]{1,0:T(8,128)S(1)} %get-tuple-element.27), channel_id=1, source_target_pairs={{0,8},{2,10},{4,12},{6,14},{8,16},{9,1},{10,18},{11,3},{12,20},{13... | collective-permute-start | bytes 3932168 | tf_op jit(solution)/shard_map/ppermute | solution.py:361
  98.6 13.3 %copy-start.3 = (f32[640,256]{1,0:T(8,128)S(1)}, f32[640,256]{1,0:T(8,128)}, u32[]{:S(2)}) copy-start(f32[640,256]{1,0:T(8,128)} %copy-done.2) | copy-start | bytes 1966084
  98.6 13.3 %copy-start.5 = (f32[640,256]{1,0:T(8,128)S(1)}, f32[640,256]{1,0:T(8,128)}, u32[]{:S(2)}) copy-start(f32[640,256]{1,0:T(8,128)} %copy-done.4) | copy-start | bytes 1966084
  113.6 19.9 %copy-start.1 = (f32[640,640]{1,0:T(8,128)S(1)}, f32[640,640]{1,0:T(8,128)}, u32[]{:S(2)}) copy-start(f32[640,640]{1,0:T(8,128)} %copy-done) | copy-start | bytes 4915204
  113.6 32.5 %collective-permute-start.13 = (f32[640,512]{1,0:T(8,128)S(1)}, f32[640,512]{1,0:T(8,128)S(1)}, u32[]{:S(2)}, u32[]{:S(2)}) collective-permute-start(f32[640,512]{1,0:T(8,128)S(1)} %add_add_fusion.loads_ref), channel_id=1, source_target_pairs={{0,8},{2,10},{4,12},{6,14},{8,16},{9,1},{10,18},{11,3},{12,20},{13... | collective-permute-start | bytes 3932168 | tf_op jit(solution)/shard_map/ppermute | solution.py:361
  141.8 8.5 %collective-permute-start.11 = (f32[320,640]{1,0:T(8,128)S(1)}, f32[320,640]{1,0:T(8,128)S(1)}, u32[]{:S(2)}, u32[]{:S(2)}) collective-permute-start(f32[320,640]{1,0:T(8,128)S(1)} %get-tuple-element.30), channel_id=1, source_target_pairs={{0,1},{1,0},{2,3},{3,2},{4,5},{5,4},{6,7},{7,6},{8,9},{9,8},{10,11... | collective-permute-start | bytes 2457608 | tf_op jit(solution)/shard_map/ppermute | solution.py:361
  148.3 4.0 %collective-permute-start.14 = (f32[640,256]{1,0:T(8,128)S(1)}, f32[640,256]{1,0:T(8,128)S(1)}, u32[]{:S(2)}, u32[]{:S(2)}) collective-permute-start(f32[640,256]{1,0:T(8,128)S(1)} %get-tuple-element.35), channel_id=1, source_target_pairs={{0,1},{1,0},{2,3},{3,2},{4,5},{5,4},{6,7},{7,6},{8,9},{9,8},{10,11... | collective-permute-start | bytes 1966088 | tf_op jit(solution)/shard_map/ppermute | solution.py:361
